TPU v7x, 32 devices: a whole 2x2x4 slice. The times are simulated.
32 devices in a mesh: groups: 2 (over y), adapter: 4 (over z), dp: 2 (over x), tensor: 2 (over core).
Axes of the slice: x: 2, y: 2, z: 4, core: 2. Of those that a mesh axis runs over, the one named last changes fastest.
Arguments:
- output_gradient: bfloat16 [4096, 4096], P(('groups', 'dp'), 'tensor'), parts along dimension 0, may hold values from -1.5 to 1.5
- hidden: bfloat16 [4096, 14336], P(('groups', 'dp'), 'adapter'), parts along dimension 0, may hold values from -6 to 6
- frozen_down_weight: bfloat16 [14336, 4096], P('adapter', 'tensor'), may hold values from -0.09375 to 0.09375
- adapter_input_panels: bfloat16 [32, 16, 14336], P(('groups', 'adapter', 'dp')), parts along dimension 0, may hold values from -0.046875 to 0.046875
- adapter_output_panels: bfloat16 [32, 16, 4096], P(('groups', 'adapter', 'dp'), None, 'tensor'), parts along dimension 0, may hold values from -0.09375 to 0.09375
- token_adapter_table: int32 [4096], P('groups'), parts along dimension 0, may hold values from 0 to 15, as said below
- adapter_slot_table: int32 [32], P('groups'), parts along dimension 0, may hold values from 0 to 15, as said below
- segment_live_tokens: int32 [32], P(('groups', 'dp')), parts along dimension 0, may hold values from 32 to 128, as said below
Outputs:
- hidden_gradient: bfloat16 [4096, 14336], P(('groups', 'dp', 'tensor'), 'adapter'), parts along dimension 0
- grad_a: float32 [32, 16, 14336], P(('groups', 'adapter', 'dp'), None, 'tensor'), parts along dimension 0
- grad_b: float32 [32, 16, 4096], P(('groups', 'adapter', 'dp'), None, 'tensor'), parts along dimension 0
There are 2 independent parts, one for each index of `groups`. A program takes and returns all parts, laid end to end along the dimension named above; an argument that names none is the same for every part. Nothing has to cross between parts.
Inputs may be any that keep to these rules, and one draw needn't show every extreme that they name: `token_adapter_table`: within each token block of 1024 tokens (one index of dp) the ids never fall. Counting slots s = adapter_slot_table[id] of the ids that one token block names, no owner block of 2 slots (s // 2) holds more than 1 distinct ones, and in every token block some owner block holds exactly 1. `adapter_slot_table`: A permutation of the slots. `segment_live_tokens`: the tokens past the live ones in a segment are padding. In every token block one segment is full, and in some token block one holds a quarter of 128.
All inputs are finite; a program needn't handle non-finite values.
Results may differ from a plain program's by a relative error of at most 0.0034.
Values may be sent and summed in bfloat16 or wider, within the bound.
A program may use at most 128 MiB of HBM per device.

v0:
```python
import jax
import jax.numpy as jnp
from jax import lax
from jax.sharding import PartitionSpec as P

adapter_scale = 4.0


def lookup(keys_row, table):
    positions = jnp.arange(table.shape[0], dtype=jnp.int32)
    picked = jnp.where(keys_row[:, None] == positions[None, :], table[None, :], 0)
    return jnp.sum(picked, axis=1)


def on_device(
    output_gradient,
    hidden,
    frozen_down_weight,
    adapter_input_panels,
    adapter_output_panels,
    token_adapter_table,
    adapter_slot_table,
    segment_live_tokens,
):
    tok_rows = output_gradient.shape[0]
    half_width = output_gradient.shape[1]
    ff_share = hidden.shape[1]
    owned_slot_list = adapter_input_panels.shape[0]
    rank_extent = adapter_input_panels.shape[1]
    n_adapter = lax.axis_size("adapter")
    n_data = lax.axis_size("dp")
    n_pair = lax.axis_size("tensor")
    capacity = owned_slot_list // 2
    owners = n_adapter * n_data
    n_slots = owners * owned_slot_list
    d_piece = half_width // n_adapter
    ff_piece = ff_share // n_pair
    half_rows = tok_rows // n_pair
    n_recv = owners * capacity
    segment_rows = tok_rows // segment_live_tokens.shape[0]
    at_adapter = lax.axis_index("adapter")
    at_data = lax.axis_index("dp")
    at_pair = lax.axis_index("tensor")
    at_owner = at_adapter * n_data + at_data
    slot_ids = jnp.arange(n_slots, dtype=jnp.int32)
    token_slot = lookup(token_adapter_table, adapter_slot_table).reshape(n_data, tok_rows)
    used_flags = jnp.any(token_slot[:, :, None] == slot_ids[None, None, :], axis=1).astype(
        jnp.int32
    )
    used_blocks = used_flags.reshape(n_data, owners, owned_slot_list)
    order_in_block = jnp.cumsum(used_blocks, axis=2) - 1
    mine_used = lax.dynamic_index_in_dim(used_blocks, at_owner, 1, False)
    mine_order = lax.dynamic_index_in_dim(order_in_block, at_owner, 1, False)
    cap_ids = jnp.arange(capacity, dtype=jnp.int32)
    picks = (mine_used[:, None, :] == 1) & (mine_order[:, None, :] == cap_ids[None, :, None])
    lower_selection = picks.astype(jnp.bfloat16)
    picks_full = picks.astype(jnp.float32)
    sent_a = jnp.einsum(
        "mjt,tou->mjou", lower_selection, adapter_input_panels, preferred_element_type=jnp.float32
    ).astype(jnp.bfloat16)
    sent_b = jnp.einsum(
        "tke,eop->tkop", lower_selection, adapter_output_panels, preferred_element_type=jnp.float32
    ).astype(jnp.bfloat16)
    sent_a = sent_a.reshape(n_data, capacity, rank_extent, n_adapter, ff_share).transpose(
        3, 0, 1, 2, 4
    )
    sent_b = sent_b.reshape(n_data, capacity, rank_extent, n_adapter, d_piece).transpose(
        3, 0, 1, 2, 4
    )
    flat_a = sent_a.reshape(n_recv, rank_extent, ff_share)
    flat_b = sent_b.reshape(n_recv, rank_extent, d_piece)
    got_a, got_b = (
        lax.all_to_all(flat_a, ("adapter", "dp"), split_axis=0, concat_axis=0, tiled=True),
        lax.all_to_all(flat_b, ("adapter", "dp"), split_axis=0, concat_axis=0, tiled=True),
    )
    panels_a = got_a.reshape(n_recv * rank_extent, ff_share)
    panels_b = got_b.reshape(n_recv * rank_extent, d_piece)
    my_slots = lax.dynamic_index_in_dim(token_slot, at_data, 0, False)
    my_order = lax.dynamic_index_in_dim(order_in_block, at_data, 0, False).reshape(n_slots)
    recv_index = my_slots // owned_slot_list * capacity + lookup(my_slots, my_order)
    recv_ids = jnp.arange(n_recv, dtype=jnp.int32)
    select = (recv_index[:, None] == recv_ids[None, :])[:, :, None]
    seg_pos = jnp.arange(segment_rows, dtype=jnp.int32)
    live_mask = (seg_pos[None, :] < segment_live_tokens[:, None]).reshape(tok_rows)
    live_grad = jnp.where(live_mask[:, None], output_gradient, jnp.zeros_like(output_gradient))
    hidden_part = lax.dynamic_slice_in_dim(hidden, at_pair * ff_piece, ff_piece, 1)
    panels_part = lax.dynamic_slice_in_dim(panels_a, at_pair * ff_piece, ff_piece, 1)
    grad_piece = lax.dynamic_slice_in_dim(live_grad, at_adapter * d_piece, d_piece, 1)
    wide_u = jnp.einsum("tf,kf->tk", hidden_part, panels_part, preferred_element_type=jnp.float32)
    wide_v = jnp.einsum("td,kd->tk", grad_piece, panels_b, preferred_element_type=jnp.float32)
    part_u = jnp.sum(jnp.where(select, wide_u.reshape(tok_rows, n_recv, rank_extent), 0.0), axis=1)
    part_v = jnp.sum(jnp.where(select, wide_v.reshape(tok_rows, n_recv, rank_extent), 0.0), axis=1)
    full_u, full_v = lax.psum((part_u, part_v), ("adapter", "tensor"))
    first_round_result = full_u.astype(jnp.bfloat16)
    second_round_result = full_v.astype(jnp.bfloat16)
    zero_low = jnp.zeros((), jnp.bfloat16)
    spread_u = jnp.where(select, first_round_result[:, None, :], zero_low).reshape(
        tok_rows, n_recv * rank_extent
    )
    spread_v = jnp.where(select, second_round_result[:, None, :], zero_low).reshape(
        tok_rows, n_recv * rank_extent
    )
    frozen_portion = lax.psum_scatter(
        jnp.einsum("td,fd->tf", live_grad, frozen_down_weight, preferred_element_type=jnp.float32),
        "tensor",
        scatter_dimension=0,
        tiled=True,
    )
    spread_half = lax.dynamic_slice_in_dim(spread_v, at_pair * half_rows, half_rows, 0)
    hidden_half = lax.dynamic_slice_in_dim(hidden, at_pair * half_rows, half_rows, 0)
    adapter_token_rows = jnp.dot(spread_half, panels_a, preferred_element_type=jnp.float32)
    hidden_gradient = (frozen_portion + adapter_scale * adapter_token_rows).astype(jnp.bfloat16)
    input_portion = adapter_scale * jnp.einsum(
        "tk,tf->kf", spread_half, hidden_half, preferred_element_type=jnp.float32
    )
    output_portion = adapter_scale * jnp.einsum(
        "tk,td->kd", spread_u, grad_piece, preferred_element_type=jnp.float32
    )
    a_width = input_portion.shape[1]
    back_a = input_portion.reshape(n_adapter, n_data, capacity, rank_extent, a_width)
    back_b = output_portion.reshape(n_adapter, n_data, capacity, rank_extent, d_piece)
    flat_back_a = back_a.reshape(n_recv, rank_extent, a_width)
    flat_back_b = back_b.reshape(n_recv, rank_extent, d_piece)
    ret_a, ret_b = (
        lax.all_to_all(flat_back_a, ("adapter", "dp"), split_axis=0, concat_axis=0, tiled=True),
        lax.all_to_all(flat_back_b, ("adapter", "dp"), split_axis=0, concat_axis=0, tiled=True),
    )
    ret_a = ret_a.reshape(n_adapter, n_data, capacity, rank_extent, a_width)
    ret_b = ret_b.reshape(n_adapter, n_data, capacity, rank_extent, d_piece)
    own_a = jnp.einsum("jcl,kjcrf->lrkf", picks_full, ret_a, precision=lax.Precision.HIGHEST)
    own_b = jnp.einsum("jcl,kjcrd->lrkd", picks_full, ret_b, precision=lax.Precision.HIGHEST)
    own_b = own_b.reshape(owned_slot_list, rank_extent, half_width)
    own_a = own_a.reshape(owned_slot_list, rank_extent, n_adapter * a_width)
    grad_a = lax.psum_scatter(own_a, "tensor", scatter_dimension=2, tiled=True)
    return (hidden_gradient, grad_a, own_b)


def solution(mesh):
    placed = (
        P(("groups", "dp"), "tensor"),
        P(("groups", "dp"), "adapter"),
        P("adapter", "tensor"),
        P(("groups", "adapter", "dp"), None, None),
        P(("groups", "adapter", "dp"), None, "tensor"),
        P("groups"),
        P("groups"),
        P(("groups", "dp")),
    )
    return jax.shard_map(
        on_device,
        mesh=mesh,
        in_specs=placed,
        out_specs=(
            P(("groups", "dp", "tensor"), "adapter"),
            P(("groups", "adapter", "dp"), None, "tensor"),
            P(("groups", "adapter", "dp"), None, "tensor"),
        ),
        check_vma=False,
    )
```

profile of v0, /device:TPU:0, one launch (start us, length us, event | category | flops | bytes accessed | tf_op | source)
XLA Modules:
  0.0 193.1 jit_solution(15983250620627803637)
XLA Ops:
  7.2 0.8 fusion.17
  8.0 2.5 %broadcast_select_fusion = bf16[1024,2048]{1,0:T(8,128)(2,1)S(1)} fusion(bf16[1024,2048]{1,0:T(8,128)(2,1)} %param.8, pred[1024]{0:T(1024)(128)(4,1)S(1)} %fusion.17), kind=kLoop, calls=%fused_computation.4 | loop fusion | flops 2097152 | bytes 8389632 | tf_op jit(solution)/shard_map/jit(_where)/select_n | solution.py:85
  10.6 2.0 %copy-done.1 = bf16[1024,2048]{1,0:T(8,128)(2,1)} copy-done((bf16[1024,2048]{1,0:T(8,128)(2,1)}, bf16[1024,2048]{1,0:T(8,128)(2,1)S(1)}, u32[]{:S(2)}) %copy-start.1) | copy-done | bytes 4194328
  12.6 21.7 %fusion.28 = f32[1024,3584]{1,0:T(8,128)} fusion(bf16[1024,2048]{1,0:T(8,128)(2,1)S(1)} %broadcast_select_fusion, bf16[3584,2048]{1,0:T(8,128)(2,1)} %param.10), kind=kOutput, calls=%fused_computation.58 | convolution fusion | flops 15032385536 | bytes 33554432 | tf_op jit(solution)/shard_map/td,fd->tf/dot_general | solution.py:104
  36.1 0.7 copy.27
  36.8 7.2 %all-to-all-start = ((bf16[8,16,512]{2,1,0:T(8,128)(2,1)}), bf16[8,16,512]{2,1,0:T(8,128)(2,1)S(1)}, u32[]{:S(2)}, u32[]{:S(2)}) async-start(bf16[8,16,512]{2,1,0:T(8,128)(2,1)} %bitcast.4), calls=%async_computation.1 | async-start | bytes 262144 | tf_op jit(solution)/shard_map/all_to_all | solution.py:74
  44.0 1.5 convolution_convert_fusion
  46.1 1.2 copy.29
  47.3 4.0 %all-to-all-done = bf16[8,16,512]{2,1,0:T(8,128)(2,1)S(1)} async-done(((bf16[8,16,512]{2,1,0:T(8,128)(2,1)}), bf16[8,16,512]{2,1,0:T(8,128)(2,1)S(1)}, u32[]{:S(2)}, u32[]{:S(2)}) %all-to-all-start) | async-done | bytes 131104 | tf_op jit(solution)/shard_map/all_to_all | solution.py:74
  51.4 3.6 %all-to-all-start.1 = ((bf16[8,16,3584]{2,1,0:T(8,128)(2,1)}), bf16[8,16,3584]{2,1,0:T(8,128)(2,1)S(1)}, u32[]{:S(2)}, u32[]{:S(2)}) async-start(bf16[8,16,3584]{2,1,0:T(8,128)(2,1)} %bitcast.7), calls=%async_computation.2 | async-start | bytes 1835008 | tf_op jit(solution)/shard_map/all_to_all | solution.py:73
  55.3 1.9 fusion.4
  57.2 19.8 %all-to-all-done.1 = bf16[8,16,3584]{2,1,0:T(8,128)(2,1)S(1)} async-done(((bf16[8,16,3584]{2,1,0:T(8,128)(2,1)}), bf16[8,16,3584]{2,1,0:T(8,128)(2,1)S(1)}, u32[]{:S(2)}, u32[]{:S(2)}) %all-to-all-start.1) | async-done | bytes 917536 | tf_op jit(solution)/shard_map/all_to_all | solution.py:73
  76.9 3.7 %fusion = f32[1024,128]{0,1:T(8,128)S(1)} fusion(bf16[1024,3584]{1,0:T(8,128)(2,1)} %param.9, s32[]{:T(128)S(6)} %select_n.76, bf16[128,3584]{1,0:T(8,128)(2,1)S(1)} %bitcast.46), kind=kOutput, calls=%fused_computation.5 | convolution fusion | flops 469762048 | bytes 4654080 | tf_op jit(solution)/shard_map/tf,kf->tk/dot_general | solution.py:89
  80.7 27.4 %all-reduce.2 = (bf16[1024,16]{0,1:T(8,128)(2,1)S(1)}, bf16[1024,16]{0,1:T(8,128)(2,1)S(1)}) all-reduce(f32[1024,16]{0,1:T(8,128)S(1)} %fusion.4, f32[1024,16]{0,1:T(8,128)S(1)} %select_reduce_fusion), channel_id=1, replica_groups=mesh['groups'=2,'adapter'=4,'dp'=2,'tensor'=2] {'adapter','tensor'}, use_global_device_ids=true, to_apply=%region_6.7 | all-reduce | flops 32768 | bytes 196608 | tf_op jit(solution)/shard_map/psum | solution.py:93
  108.1 2.7 %convolution_multiply_fusion = f32[128,3584]{1,0:T(8,128)S(1)} fusion(bf16[1024,3584]{1,0:T(8,128)(2,1)} %param.9, s32[]{:T(128)S(6)} %select_n.75, bf16[1024,128]{0,1:T(8,128)(2,1)S(1)} %bitcast.49), kind=kOutput, calls=%fused_computation.2 | convolution fusion | flops 470220800 | bytes 5637120 | tf_op jit(solution)/shard_map/tk,tf->kf/dot_general | solution.py:113
  110.8 46.1 %all_to_all.20 = f32[8,16,3584]{2,1,0:T(8,128)S(1)} all-to-all(f32[8,16,3584]{2,1,0:T(8,128)S(1)} %bitcast.45), channel_id=1, replica_groups=mesh['groups'=2,'adapter'=4,'dp'=2,'tensor'=2] {'adapter','dp'}, dimensions={0} | all-to-all | bytes 3670016 | tf_op jit(solution)/shard_map/all_to_all | solution.py:125
  156.9 4.2 %convolution_bitcast_fusion = f32[2,16,4,3584]{3,0,1,2:T(2,128)S(1)} fusion(f32[4,2,16,3584]{3,2,1,0:T(8,128)S(1)} %bitcast.48, pred[2,1,2]{2,0,1:T(4,128)(4,1)S(1)} %copy.40), kind=kOutput, calls=%fused_computation.3 | convolution fusion | flops 11010048 | bytes 3670020 | tf_op jit(solution)/shard_map/jcl,kjcrf->lrkf/dot_general | solution.py:130
  161.1 1.2 copy.32
  162.3 2.5 %reshape.156 = f32[2,16,14336]{2,1,0:T(8,128)} reshape(f32[2,16,4,3584]{3,2,1,0:T(4,128)S(1)} %copy.32) | data formatting | bytes 3670016 | tf_op jit(solution)/shard_map/reshape | solution.py:133
  164.8 1.6 convolution_multiply_fusion.1
  166.4 12.0 %all_to_all.21 = f32[8,16,512]{2,1,0:T(8,128)S(1)} all-to-all(f32[8,16,512]{2,1,0:T(8,128)S(1)} %bitcast.53), channel_id=1, replica_groups=mesh['groups'=2,'adapter'=4,'dp'=2,'tensor'=2] {'adapter','dp'}, dimensions={0} | all-to-all | bytes 524288 | tf_op jit(solution)/shard_map/all_to_all | solution.py:126
  178.4 0.7 convolution_bitcast_fusion.1
  179.3 0.9 reshape.159
  180.2 6.1 %add_convert_fusion = bf16[512,3584]{1,0:T(8,128)(2,1)} fusion(f32[512,3584]{1,0:T(8,128)} %reduce-scatter.3.cloned.1.call-done, bf16[128,3584]{1,0:T(8,128)(2,1)S(1)} %bitcast.47, bf16[1024,128]{0,1:T(8,128)(2,1)S(1)} %bitcast.50, s32[]{:T(128)S(6)} %select_n.75), kind=kOutput, calls=%fused_computation.1 | convolution fusion | flops 475267072 | bytes 12058628 | tf_op jit(solution)/shard_map/dot_general | solution.py:111
  (40 shorter events, 2.9 us)
Async XLA Ops:
  7.2 36.9 %copy-start = (bf16[2,16,14336]{2,1,0:T(8,128)(2,1)S(1)}, bf16[2,16,14336]{2,1,0:T(8,128)(2,1)}, u32[]{:S(2)}) copy-start(bf16[2,16,14336]{2,1,0:T(8,128)(2,1)} %param.11) | copy-start | bytes 2752516
  7.2 173.0 %reduce-scatter.3.cloned.1.call-start = ((), (), s32[]{:S(2)}) async-start(), calls=%async_computation.6 | async-start | bytes 22020096 | tf_op jit(solution)/shard_map/reduce_scatter | solution.py:103
  10.6 2.0 %copy-start.1 = (bf16[1024,2048]{1,0:T(8,128)(2,1)}, bf16[1024,2048]{1,0:T(8,128)(2,1)S(1)}, u32[]{:S(2)}) copy-start(bf16[1024,2048]{1,0:T(8,128)(2,1)S(1)} %broadcast_select_fusion) | copy-start | bytes 12582916
  34.3 0.7 copy-start.4
  34.3 0.7 copy-start.5
  34.3 1.4 copy-start.6
  36.8 14.6 %all-to-all-start = ((bf16[8,16,512]{2,1,0:T(8,128)(2,1)}), bf16[8,16,512]{2,1,0:T(8,128)(2,1)S(1)}, u32[]{:S(2)}, u32[]{:S(2)}) async-start(bf16[8,16,512]{2,1,0:T(8,128)(2,1)} %bitcast.4), calls=%async_computation.1 | async-start | bytes 262144 | tf_op jit(solution)/shard_map/all_to_all | solution.py:74
  51.4 25.6 %all-to-all-start.1 = ((bf16[8,16,3584]{2,1,0:T(8,128)(2,1)}), bf16[8,16,3584]{2,1,0:T(8,128)(2,1)S(1)}, u32[]{:S(2)}, u32[]{:S(2)}) async-start(bf16[8,16,3584]{2,1,0:T(8,128)(2,1)} %bitcast.7), calls=%async_computation.2 | async-start | bytes 1835008 | tf_op jit(solution)/shard_map/all_to_all | solution.py:73
  55.0 131.3 %reduce-scatter.5.cloned.1.call-start = ((), (), s32[]{:S(2)}) async-start(), calls=%async_computation.7 | async-start | bytes 2752512 | tf_op jit(solution)/shard_map/reduce_scatter | solution.py:134
  76.9 33.9 %copy-start.2 = (bf16[8,16,3584]{2,1,0:T(8,128)(2,1)}, bf16[8,16,3584]{2,1,0:T(8,128)(2,1)S(1)}, u32[]{:S(2)}) copy-start(bf16[8,16,3584]{2,1,0:T(8,128)(2,1)S(1)} %all-to-all-done.1) | copy-start | bytes 2752516
  164.8 15.4 %copy-start.3 = (bf16[8,16,3584]{2,1,0:T(8,128)(2,1)S(1)}, bf16[8,16,3584]{2,1,0:T(8,128)(2,1)}, u32[]{:S(2)}) copy-start(bf16[8,16,3584]{2,1,0:T(8,128)(2,1)} %copy-done.2) | copy-start | bytes 2752516
Sparse Core Ops, SparseCore 0:
  34.5 26.7 reduce-scatter.2
  164.9 8.4 reduce-scatter.4
where the time goes:
time: 194 us; the launch traced here: 193 us
  blocking collectives  85.4 us (44%)
  matrix products  44.3 us (23%)
  waiting for transfers between devices  23.9 us (12%)
  between operations  14.3 us (7%)
  starting transfers between devices  10.9 us (6%)
  local copies, waits for them, and re-layouts  10.2 us (5%)
  other arithmetic  4.12 us (2%)
    all_to_all x1, blocking collectives, on_device(): lax.all_to_all(flat_back_a, ('adapter', 'dp'), split_axis=0, concat_axis=...  46.1 us
    psum x1, blocking collectives, on_device(): full_u, full_v = lax.psum((part_u, part_v), ('adapter', 'tensor'))  27.4 us
    dot_general x1, matrix products, on_device(): jnp.einsum('td,fd->tf', live_grad, frozen_down_weight, preferred_element_...  21.7 us
    all_to_all x1, waiting for transfers between devices, on_device(): lax.all_to_all(flat_a, ('adapter', 'dp'), split_axis=0, concat_axis=0, ti...  19.8 us
    all_to_all x1, blocking collectives, on_device(): lax.all_to_all(flat_back_b, ('adapter', 'dp'), split_axis=0, concat_axis=...  12 us
    all_to_all x1, starting transfers between devices, on_device(): lax.all_to_all(flat_b, ('adapter', 'dp'), split_axis=0, concat_axis=0, ti...  7.25 us
    dot_general x1, matrix products, on_device(): jnp.dot(spread_half, panels_a, preferred_element_type=jnp.float32)  6.06 us
    dot_general x1, matrix products, on_device(): jnp.einsum('jcl,kjcrf->lrkf', picks_full, ret_a, precision=lax.Precision....  4.18 us
  transfers between devices with their start and end apart: 4, of which 2 were waited for; matrix products, arithmetic and copies ran while one was open for 16% of the time, Pallas kernels for 0%

commit v1 on v0

--- a/solution.py
+++ b/solution.py
@@ -1,9 +1,16 @@
+import functools
+
 import jax
 import jax.numpy as jnp
 from jax import lax
+from jax.experimental import pallas as pl
+from jax.experimental.pallas import tpu as pltpu
 from jax.sharding import PartitionSpec as P
 
 adapter_scale = 4.0
+MESH = pl.DeviceIdType.MESH
+NT = (((1,), (1,)), ((), ()))
+TILE = 256
 
 
 def lookup(keys_row, table):
@@ -12,7 +19,7 @@
     return jnp.sum(picked, axis=1)
 
 
-def on_device(
+def plain_on_device(
     output_gradient,
     hidden,
     frozen_down_weight,
@@ -135,6 +142,564 @@
     return (hidden_gradient, grad_a, own_b)
 
 
+def fused_kernel(
+    sizes,
+    grad_hbm,
+    hidden_hbm,
+    weight_hbm,
+    sent_a_hbm,
+    sent_b_hbm,
+    choose_ref,
+    choose_mine_ref,
+    live_ref,
+    pick_ref,
+    out_hbm,
+    grad_a_ref,
+    grad_b_ref,
+    grad,
+    hid,
+    weight,
+    panels_a,
+    panels_b,
+    own_acc,
+    to_pair,
+    from_pair,
+    staged,
+    part,
+    part_in,
+    low,
+    spread,
+    spread_own,
+    piece_a,
+    back_a,
+    piece_b,
+    back_b,
+    load_sem,
+    weight_sem,
+    out_sem,
+    a_send,
+    a_recv,
+    b_send,
+    b_recv,
+    pair_send,
+    pair_recv,
+    fwd_sem,
+    rs_send,
+    rs_recv,
+    ag_send,
+    ag_recv,
+    ra_send,
+    ra_recv,
+    rb_send,
+    rb_recv,
+):
+    n_adapter, n_data, n_pair, rank = sizes
+    tok, width = grad.shape
+    half = tok // n_pair
+    ff_half = hid.shape[1]
+    ff = ff_half * n_pair
+    n_own = n_adapter * n_data
+    n_sum = n_adapter * n_pair
+    tok_piece = tok // n_sum
+    n_tile = ff // TILE
+    at_g = lax.axis_index("groups")
+    at_a = lax.axis_index("adapter")
+    at_d = lax.axis_index("dp")
+    at_t = lax.axis_index("tensor")
+    at_own = at_a * n_data + at_d
+    at_sum = at_a * n_pair + at_t
+
+    def dev(a, d, t):
+        return (at_g, a, d, t)
+
+    def remote(src, dst, send, recv, to):
+        return pltpu.make_async_remote_copy(
+            src_ref=src, dst_ref=dst, send_sem=send, recv_sem=recv, device_id=to, device_id_type=MESH
+        )
+
+    def lanes(start, size):
+        return pl.ds(pl.multiple_of(start, 128), size)
+
+    def rows(start, size):
+        return pl.ds(pl.multiple_of(start, 16), size)
+
+    load_grad = pltpu.make_async_copy(grad_hbm, grad, load_sem.at[0])
+    load_hid = pltpu.make_async_copy(
+        hidden_hbm.at[:, lanes(at_t * ff_half, ff_half)], hid, load_sem.at[1]
+    )
+    load_grad.start()
+
+    def load_weight(c):
+        place = pl.ds(pl.multiple_of(c * TILE, TILE), TILE)
+        return pltpu.make_async_copy(weight_hbm.at[place, :], weight.at[place, :], weight_sem.at[c])
+
+    def start_weight(c, _):
+        load_weight(c).start()
+        return 0
+
+    load_weight(0).start()
+    load_weight(1).start()
+
+    at_all = at_own * n_pair + at_t
+    n_all = n_own * n_pair
+    barrier = pltpu.get_barrier_semaphore()
+
+    def greet(k, _):
+        i = lax.rem(at_all + k, n_all)
+        pl.semaphore_signal(
+            barrier,
+            inc=1,
+            device_id=dev(
+                lax.div(i, n_data * n_pair), lax.rem(lax.div(i, n_pair), n_data), lax.rem(i, n_pair)
+            ),
+            device_id_type=MESH,
+        )
+        return 0
+
+    lax.fori_loop(1, n_all, greet, 0)
+    pl.semaphore_wait(barrier, n_all - 1)
+
+    b_copies = [
+        pltpu.make_async_copy(
+            sent_b_hbm.at[at_d], panels_b.at[rows(at_d * rank, rank), :], load_sem.at[2]
+        )
+    ]
+    for k in range(1, n_data):
+        j = lax.rem(at_d + k, n_data)
+        b_copies.append(
+            remote(
+                sent_b_hbm.at[j],
+                panels_b.at[rows(at_d * rank, rank), :],
+                b_send.at[k],
+                b_recv.at[k],
+                dev(at_a, j, at_t),
+            )
+        )
+    for copy in b_copies:
+        copy.start()
+
+    mine = lanes(at_t * ff_half, ff_half)
+    a_copies = [
+        pltpu.make_async_copy(
+            sent_a_hbm.at[at_d, :, lanes(at_a * ff + at_t * ff_half, ff_half)],
+            panels_a.at[rows(at_own * rank, rank), mine],
+            load_sem.at[3],
+        )
+    ]
+    for k in range(1, n_own):
+        o = lax.rem(at_own + k, n_own)
+        a2, d2 = lax.div(o, n_data), lax.rem(o, n_data)
+        a_copies.append(
+            remote(
+                sent_a_hbm.at[d2, :, lanes(a2 * ff + at_t * ff_half, ff_half)],
+                panels_a.at[rows(at_own * rank, rank), mine],
+                a_send.at[k],
+                a_recv.at[k],
+                dev(a2, d2, at_t),
+            )
+        )
+    for copy in a_copies:
+        copy.start()
+    lax.fori_loop(2, 6, start_weight, 0)
+    load_hid.start()
+    lax.fori_loop(6, n_tile, start_weight, 0)
+    load_grad.wait()
+
+    pair_dev = dev(at_a, at_d, 1 - at_t)
+    mine_rows = pl.ds(pl.multiple_of(at_t * half, half), half)
+    pair_rows = pl.ds(pl.multiple_of((1 - at_t) * half, half), half)
+
+    def pair_copy(c):
+        return remote(to_pair.at[c], from_pair.at[c], pair_send.at[c], pair_recv.at[c], pair_dev)
+
+    forward = remote(
+        panels_a.at[:, mine], panels_a.at[:, mine], fwd_sem.at[0], fwd_sem.at[1], pair_dev
+    )
+
+    def sum_peer(k):
+        q = lax.rem(at_sum + k, n_sum)
+        return q, dev(lax.div(q, n_pair), at_d, lax.rem(q, n_pair))
+
+    def scatter_copies(w):
+        copies = []
+        for k in range(1, n_sum):
+            q, to = sum_peer(k)
+            copies.append(
+                remote(
+                    part.at[w, q], part_in.at[w, k], rs_send.at[w, k], rs_recv.at[w, k], to
+                )
+            )
+        return copies
+
+    def gather_copies(w):
+        copies = []
+        for k in range(1, n_sum):
+            _, to = sum_peer(k)
+            copies.append(
+                remote(
+                    low.at[w, at_sum], low.at[w, at_sum], ag_send.at[w, k], ag_recv.at[w, k], to
+                )
+            )
+        return copies
+
+    def start_all(copies):
+        for copy in copies:
+            copy.start()
+
+    def wait_all(copies):
+        for copy in copies:
+            copy.wait()
+
+    def store_part(w, i, value):
+        for s in range(TILE // tok_piece):
+            part[w, i * (TILE // tok_piece) + s] = value[:, s * tok_piece : (s + 1) * tok_piece]
+
+    def part_v():
+        wait_all(b_copies)
+
+        def step(i, _):
+            block = grad[pl.ds(pl.multiple_of(i * TILE, TILE), TILE), :]
+            wide = lax.dot_general(panels_b[...], block, NT, preferred_element_type=jnp.float32)
+            total = jnp.zeros((rank, TILE), jnp.float32)
+            for j in range(n_data):
+                keep = choose_mine_ref[j : j + 1, lanes(i * TILE, TILE)]
+                total += wide[j * rank : (j + 1) * rank] * keep
+            store_part(1, i, total)
+            return 0
+
+        lax.fori_loop(0, tok // TILE, step, 0)
+        start_all(scatter_copies(1))
+
+    def part_u():
+        wait_all(a_copies)
+        forward.start()
+
+        def step(i, _):
+            block = hid[pl.ds(pl.multiple_of(i * TILE, TILE), TILE), :]
+            wide = lax.dot_general(
+                panels_a[:, mine], block, NT, preferred_element_type=jnp.float32
+            )
+            total = jnp.zeros((rank, TILE), jnp.float32)
+            for o in range(n_own):
+                keep = choose_ref[o : o + 1, lanes(i * TILE, TILE)]
+                total += wide[o * rank : (o + 1) * rank] * keep
+            store_part(0, i, total)
+            return 0
+
+        lax.fori_loop(0, tok // TILE, step, 0)
+        start_all(scatter_copies(0))
+
+    def sum_low(w):
+        wait_all(scatter_copies(w))
+        total = part[w, at_sum]
+        for k in range(1, n_sum):
+            total += part_in[w, k]
+        low[w, at_sum] = total.astype(jnp.bfloat16)
+        start_all(gather_copies(w))
+
+    def use_v():
+        wait_all(gather_copies(1))
+        for i in range(n_sum):
+            value = low[1, i].astype(jnp.float32) * adapter_scale
+            place = slice(i * tok_piece, (i + 1) * tok_piece)
+            for o in range(n_own):
+                spread[o * rank : (o + 1) * rank, place] = (
+                    value * choose_ref[o : o + 1, place]
+                ).astype(jnp.bfloat16)
+        load_hid.wait()
+
+        def step(i, _):
+            place = lanes(i * TILE, TILE)
+            piece_a[:, place] = jnp.dot(
+                spread[...], hid[:, place], preferred_element_type=jnp.float32
+            ).astype(jnp.bfloat16)
+            return 0
+
+        lax.fori_loop(0, ff_half // TILE, step, 0)
+        spread_own[...] = jnp.transpose(
+            spread[:, lanes(at_t * half, half)].astype(jnp.float32)
+        ).astype(jnp.bfloat16)
+        return_a(True)
+
+    ratio = n_adapter // n_pair
+    core = lax.div(at_a, ratio)
+    low_a = lax.rem(at_a, ratio)
+    ret_slot = (low_a * n_data + at_d) * n_pair + at_t
+    ret_place = lanes(low_a * ff + at_t * ff_half, ff_half)
+
+    def return_copy(k):
+        o = lax.rem(at_own + k, n_own)
+        return remote(
+            piece_a.at[rows(o * rank, rank), :],
+            back_a.at[at_d, :, ret_place],
+            ra_send.at[k],
+            ra_recv.at[ret_slot],
+            dev(lax.div(o, n_data), lax.rem(o, n_data), core),
+        )
+
+    def return_a(start):
+        for k in range(1, n_own):
+            if start:
+                return_copy(k).start()
+            else:
+                return_copy(k).wait_send()
+
+        @pl.when(at_t != core)
+        def _():
+            if start:
+                return_copy(0).start()
+            else:
+                return_copy(0).wait_send()
+
+        if start:
+
+            @pl.when(at_t == core)
+            def _():
+                pltpu.make_async_copy(
+                    piece_a.at[rows(at_own * rank, rank), :],
+                    back_a.at[at_d, :, ret_place],
+                    ra_recv.at[ret_slot],
+                ).start()
+
+    def wait_returned():
+        for s in range(ratio * n_data * n_pair):
+            a2, d2, t2 = s // (n_data * n_pair), s // n_pair % n_data, s % n_pair
+            first = a2 * ff + t2 * ff_half
+            place = back_a.at[d2, :, first : first + ff_half]
+            remote(place, place, ra_send.at[0], ra_recv.at[s], pair_dev).wait_recv()
+
+    def return_b():
+        copies = []
+        for k in range(1, n_data):
+            j = lax.rem(at_d + k, n_data)
+            copies.append(
+                remote(
+                    piece_b.at[j], back_b.at[k], rb_send.at[k], rb_recv.at[k], dev(at_a, j, at_t)
+                )
+            )
+        return copies
+
+    def use_u():
+        wait_all(gather_copies(0))
+        parts = []
+        for i in range(n_sum):
+            value = low[0, i].astype(jnp.float32) * adapter_scale
+            place = slice(i * tok_piece, (i + 1) * tok_piece)
+            parts.append(
+                jnp.concatenate(
+                    [
+                        value * choose_mine_ref[j : j + 1, place]
+                        for j in range(n_data)
+                    ],
+                    axis=0,
+                ).astype(jnp.bfloat16)
+            )
+        spread_u = jnp.concatenate(parts, axis=1)
+        for i in range(width // 512):
+            place = slice(i * 512, (i + 1) * 512)
+            wide = jnp.dot(spread_u, grad[:, place], preferred_element_type=jnp.float32)
+            for j in range(n_data):
+                piece_b[j, :, place] = wide[j * rank : (j + 1) * rank]
+        start_all(return_b())
+
+    events = {
+        1: part_v,
+        3: lambda: sum_low(1),
+        5: use_v,
+        7: part_u,
+        9: lambda: sum_low(0),
+        11: use_u,
+    }
+
+    def main(c, _):
+        load_weight(c).wait()
+        w = weight[pl.ds(pl.multiple_of(c * TILE, TILE), TILE), :]
+        to_pair[c] = lax.dot_general(
+            grad[pair_rows, :], w, NT, preferred_element_type=jnp.float32
+        ).astype(jnp.bfloat16)
+        pair_copy(c).start()
+        own_acc[c] = lax.dot_general(grad[mine_rows, :], w, NT, preferred_element_type=jnp.float32)
+        for at, event in events.items():
+            pl.when(c == min(at, n_tile - 1))(event)
+        return 0
+
+    lax.fori_loop(0, n_tile, main, 0)
+    forward.wait()
+
+    def store_copy(c):
+        return pltpu.make_async_copy(staged.at[c], out_hbm.at[:, lanes(c * TILE, TILE)], out_sem.at[c])
+
+    def finish(c, _):
+        pair_copy(c).wait()
+        total = own_acc[c] + from_pair[c].astype(jnp.float32)
+        total += jnp.dot(
+            spread_own[...], panels_a[:, lanes(c * TILE, TILE)], preferred_element_type=jnp.float32
+        )
+        staged[c] = jnp.where(live_ref[...] > 0, total, 0.0).astype(jnp.bfloat16)
+        store_copy(c).start()
+        return 0
+
+    lax.fori_loop(0, n_tile, finish, 0)
+
+    wait_all(return_b())
+    n_slot = grad_b_ref.shape[0]
+    for l in range(n_slot):
+        total = piece_b[at_d] * pick_ref[at_d, l]
+        for k in range(1, n_data):
+            total += back_b[k] * pick_ref[lax.rem(at_d + n_data - k, n_data), l]
+        grad_b_ref[l] = total
+    return_a(False)
+    wait_returned()
+    for l in range(n_slot):
+        total = back_a[0].astype(jnp.float32) * pick_ref[0, l]
+        for d in range(1, n_data):
+            total += back_a[d].astype(jnp.float32) * pick_ref[d, l]
+        grad_a_ref[l] = total
+
+    def drain(c, _):
+        store_copy(c).wait()
+        return 0
+
+    lax.fori_loop(0, n_tile, drain, 0)
+
+
+def fused_on_device(
+    output_gradient,
+    hidden,
+    frozen_down_weight,
+    adapter_input_panels,
+    adapter_output_panels,
+    token_adapter_table,
+    adapter_slot_table,
+    segment_live_tokens,
+):
+    tok, width = output_gradient.shape
+    ff = hidden.shape[1]
+    n_slot, rank, ff_all = adapter_input_panels.shape
+    n_adapter = lax.axis_size("adapter")
+    n_data = lax.axis_size("dp")
+    n_pair = lax.axis_size("tensor")
+    n_own = n_adapter * n_data
+    n_sum = n_adapter * n_pair
+    half = tok // n_pair
+    ff_half = ff // n_pair
+    n_tile = ff // TILE
+    at_data = lax.axis_index("dp")
+    at_pair = lax.axis_index("tensor")
+    at_own = lax.axis_index("adapter") * n_data + at_data
+    token_slot = lookup(token_adapter_table, adapter_slot_table).reshape(n_data, tok)
+    my_ids = at_own * n_slot + jnp.arange(n_slot, dtype=jnp.int32)
+    pick = jnp.any(token_slot[:, :, None] == my_ids[None, None, :], axis=1)
+    sent_a = jnp.zeros((n_data, rank, ff_all), jnp.bfloat16)
+    sent_b = jnp.zeros((n_data, rank, width), jnp.bfloat16)
+    for l in range(n_slot):
+        sent_a = jnp.where(pick[:, l, None, None], adapter_input_panels[l][None], sent_a)
+        sent_b = jnp.where(pick[:, l, None, None], adapter_output_panels[l][None], sent_b)
+    seg = tok // segment_live_tokens.shape[0]
+    seg_pos = jnp.arange(seg, dtype=jnp.int32)
+    live = (seg_pos[None, :] < segment_live_tokens[:, None]).reshape(tok)
+    my_owner = lax.dynamic_index_in_dim(token_slot, at_data, 0, False) // n_slot
+    owner_ids = jnp.arange(n_own, dtype=jnp.int32)
+    choose = ((my_owner[None, :] == owner_ids[:, None]) & live[None, :]).astype(jnp.float32)
+    choose_mine = lax.dynamic_slice_in_dim(choose, at_own - at_data, n_data, 0)
+    live_half = lax.dynamic_slice_in_dim(live, at_pair * half, half, 0).astype(jnp.float32)[:, None]
+    anywhere = pl.BlockSpec(memory_space=pl.ANY)
+    vmem = pl.BlockSpec(memory_space=pltpu.VMEM)
+    dma = pltpu.SemaphoreType.DMA
+    bf16, f32 = jnp.bfloat16, jnp.float32
+    ff_out = ff_all // n_pair
+    n_back = n_adapter // n_pair * n_data * n_pair
+    return pl.pallas_call(
+        functools.partial(fused_kernel, (n_adapter, n_data, n_pair, rank)),
+        out_shape=(
+            jax.ShapeDtypeStruct((half, ff), bf16),
+            jax.ShapeDtypeStruct((n_slot, rank, ff_out), f32),
+            jax.ShapeDtypeStruct((n_slot, rank, width), f32),
+        ),
+        in_specs=[anywhere] * 5 + [vmem, vmem, vmem, pl.BlockSpec(memory_space=pltpu.SMEM)],
+        out_specs=(anywhere, vmem, vmem),
+        scratch_shapes=[
+            pltpu.VMEM((tok, width), bf16),
+            pltpu.VMEM((tok, ff_half), bf16),
+            pltpu.VMEM((ff, width), bf16),
+            pltpu.VMEM((n_own * rank, ff), bf16),
+            pltpu.VMEM((n_data * rank, width), bf16),
+            pltpu.VMEM((n_tile, half, TILE), f32),
+            pltpu.VMEM((n_tile, half, TILE), bf16),
+            pltpu.VMEM((n_tile, half, TILE), bf16),
+            pltpu.VMEM((n_tile, half, TILE), bf16),
+            pltpu.VMEM((2, n_sum, rank, tok // n_sum), f32),
+            pltpu.VMEM((2, n_sum, rank, tok // n_sum), f32),
+            pltpu.VMEM((2, n_sum, rank, tok // n_sum), bf16),
+            pltpu.VMEM((n_own * rank, tok), bf16),
+            pltpu.VMEM((half, n_own * rank), bf16),
+            pltpu.VMEM((n_own * rank, ff_half), bf16),
+            pltpu.VMEM((n_data, rank, ff_out), bf16),
+            pltpu.VMEM((n_data, rank, width), f32),
+            pltpu.VMEM((n_data, rank, width), f32),
+            dma((4,)),
+            dma((n_tile,)),
+            dma((n_tile,)),
+            dma((n_own,)),
+            dma((n_own,)),
+            dma((n_data,)),
+            dma((n_data,)),
+            dma((n_tile,)),
+            dma((n_tile,)),
+            dma((2,)),
+            dma((2, n_sum)),
+            dma((2, n_sum)),
+            dma((2, n_sum)),
+            dma((2, n_sum)),
+            dma((n_own,)),
+            dma((n_back,)),
+            dma((n_data,)),
+            dma((n_data,)),
+        ],
+        compiler_params=pltpu.CompilerParams(
+            collective_id=0, has_side_effects=True, vmem_limit_bytes=60 * 1024 * 1024
+        ),
+        cost_estimate=pl.CostEstimate(
+            flops=2 * tok * width * ff, bytes_accessed=2 * ff * width, transcendentals=0
+        ),
+    )(
+        output_gradient,
+        hidden,
+        frozen_down_weight,
+        sent_a,
+        sent_b,
+        choose,
+        choose_mine,
+        live_half,
+        pick.astype(jnp.float32),
+    )
+
+
+def fits_kernel(hidden, adapter_input_panels):
+    ff = hidden.shape[1]
+    n_slot, rank, _ = adapter_input_panels.shape
+    n_adapter = lax.axis_size("adapter")
+    n_data = lax.axis_size("dp")
+    n_pair = lax.axis_size("tensor")
+    n_sum = n_adapter * n_pair
+    return (
+        n_pair == 2
+        and n_slot == 2
+        and rank == 16
+        and n_adapter % n_pair == 0
+        and ff % (n_pair * TILE) == 0
+        and ff // TILE > 11
+        and hidden.shape[0] == n_sum * 128
+        and n_adapter * n_data * rank <= 256
+    )
+
+
+def on_device(*args):
+    if fits_kernel(args[1], args[3]):
+        return fused_on_device(*args)
+    return plain_on_device(*args)
+
+
 def solution(mesh):
     placed = (
         P(("groups", "dp"), "tensor"),

time: 194 us -> 72.4 us (0.37)
  blocking collectives: 85.4 us -> 0 us
  Pallas kernels: 0 us -> 57.6 us
  matrix products: 44.3 us -> 0 us
  waiting for transfers between devices: 23.9 us -> 0 us
  between operations: 14.3 us -> 0.72 us
  starting transfers between devices: 10.9 us -> 0 us
    all_to_all x2 -> x0, blocking collectives: 58.1 us -> none  [the longest x1 46.1 us: on_device(): lax.all_to_all(flat_back_a, ('adapter', 'dp'), split_axis=0, concat_axis=...]
    pallas_call x0 -> x1, Pallas kernels: none -> 57.6 us  [fused_on_device(): pl.pallas_call(functools.partial(fused_kernel, (n_adapter, n_data, n_pair...]
    dot_general x10 -> x0, matrix products: 44.3 us -> none  [the longest x1 21.7 us: on_device(): jnp.einsum('td,fd->tf', live_grad, frozen_down_weight, preferred_element_...]
    psum x1 -> x0, blocking collectives: 27.4 us -> none  [on_device(): full_u, full_v = lax.psum((part_u, part_v), ('adapter', 'tensor'))]
    all_to_all x2 -> x0, waiting for transfers between devices: 23.8 us -> none  [the longest x1 19.8 us: on_device(): lax.all_to_all(flat_a, ('adapter', 'dp'), split_axis=0, concat_axis=0, ti...]
    all_to_all x2 -> x0, starting transfers between devices: 10.8 us -> none  [the longest x1 7.25 us: on_device(): lax.all_to_all(flat_b, ('adapter', 'dp'), split_axis=0, concat_axis=0, ti...]
    reshape x6 -> x0, local copies, waits for them, and re-layouts: 5.24 us -> none  [the longest x1 2.48 us: on_device(): own_a = own_a.reshape(owned_slot_list, rank_extent, n_adapter * a_width)]
    unnamed x15 -> x9, local copies, waits for them, and re-layouts: 2.69 us -> 5.84 us
  transfers between devices with their start and end apart: 4 -> 0, of which waited for: 2 -> 0; matrix products, arithmetic and copies ran while one was open for 16% -> 0% of each run, Pallas kernels for 0% -> 0%
where the time goes in v1:
time: 72.4 us; the launch traced here: 72.2 us
  Pallas kernels  57.6 us (80%)
  local copies, waits for them, and re-layouts  9.59 us (13%)
  other arithmetic  4.25 us (6%)
    pallas_call x1, Pallas kernels, fused_on_device(): pl.pallas_call(functools.partial(fused_kernel, (n_adapter, n_data, n_pair...  57.6 us
    unnamed x9, local copies, waits for them, and re-layouts  5.84 us

profile of v1, /device:TPU:0, one launch (start us, length us, event | category | flops | bytes accessed | tf_op | source)
XLA Modules:
  0.0 72.2 jit_solution(5715751593220439837)
XLA Ops:
  0.7 0.7 %fusion.2 = pred[1024]{0:T(1024)(128)(4,1)S(1)} fusion(s32[8]{0:T(128)} %param.15), kind=kLoop, calls=%fused_computation.17 | loop fusion | flops 1024 | bytes 1056 | tf_op jit(solution)/shard_map/lt | solution.py:600
  1.4 0.1 dynamic-slice_convert_fusion
  1.5 0.8 %select_reduce_fusion = s32[2048]{0:T(1024)S(1)} fusion(s32[16]{0:T(128)} %param.14, s32[2048]{0:T(1024)} %param.13), kind=kLoop, calls=%fused_computation.4 | loop fusion | flops 96256 | bytes 16448 | tf_op jit(solution)/shard_map/reduce_sum | solution.py:19
  2.3 0.2 compare_reduce_fusion
  2.5 0.6 convert_element_type.8.pick_ref
  3.1 0.2 slice_reduce_fusion.1
  3.3 0.0 copy-start.2
  3.3 0.6 constant_dynamic-slice_fusion.choose_mine_ref
  3.9 0.9 %slice_bitcast_fusion.3 = (bf16[16,2048]{1,0:T(8,128)(2,1)S(1)}, bf16[16,2048]{1,0:T(8,128)(2,1)S(1)}) fusion(bf16[2,16,2048]{2,1,0:T(8,128)(2,1)} %param.12), kind=kLoop, calls=%fused_computation.7 | loop fusion | bytes 262144 | tf_op jit(solution)/shard_map/jit(_where)/broadcast_in_dim | solution.py:597
  4.8 0.7 %select_select_fusion.1.sent_b_hbm = bf16[2,16,2048]{2,1,0:T(8,128)(2,1)} fusion(pred[2]{0:T(512)(128)(4,1)S(1)} %get-tuple-element.4, pred[2]{0:T(512)(128)(4,1)S(1)} %get-tuple-element.3, bf16[16,2048]{1,0:T(8,128)(2,1)S(1)} %get-tuple-element.8, bf16[16,2048]{1,0:T(8,128)(2,1)S(1)} %get-tuple-element.7), kind=kLoop, calls=%fused_computation.3 | loop fusion | flops 131072 | bytes 262148 | tf_op jit(solution)/shard_map/jit(_where)/select_n | solution.py:597
  5.5 0.9 %copy.12.live_ref = f32[512,1]{1,0:T(8,128)} copy(f32[512,1]{0,1:T(1,128)S(1)} %bitcast.13) | data formatting | bytes 4096 | tf_op jit(solution)/shard_map/broadcast_in_dim | solution.py:605
  6.4 1.2 %slice_bitcast_fusion.1 = (bf16[16,14336]{1,0:T(8,128)(2,1)S(1)}, bf16[16,14336]{1,0:T(8,128)(2,1)S(1)}) fusion(bf16[2,16,14336]{2,1,0:T(8,128)(2,1)} %param.11), kind=kLoop, calls=%fused_computation.2 | loop fusion | bytes 1835008 | tf_op jit(solution)/shard_map/jit(_where)/broadcast_in_dim | solution.py:596
  7.6 1.1 %select_select_fusion.sent_a_hbm = bf16[2,16,14336]{2,1,0:T(8,128)(2,1)} fusion(pred[2]{0:T(512)(128)(4,1)S(1)} %get-tuple-element.4, pred[2]{0:T(512)(128)(4,1)S(1)} %get-tuple-element.3, bf16[16,14336]{1,0:T(8,128)(2,1)S(1)} %get-tuple-element.6, bf16[16,14336]{1,0:T(8,128)(2,1)S(1)} %get-tuple-element.5), kind=kLoop, calls=%fused_computation | loop fusion | flops 917504 | bytes 1835012 | tf_op jit(solution)/shard_map/jit(_where)/select_n | solution.py:596
  8.7 0.0 copy-done.2
  8.7 57.6 %shard_map.103 = (bf16[512,3584]{1,0:T(8,128)(2,1)}, f32[2,16,7168]{2,1,0:T(8,128)}, f32[2,16,2048]{2,1,0:T(8,128)}) custom-call(bf16[1024,2048]{1,0:T(8,128)(2,1)} %grad_hbm.1, bf16[1024,3584]{1,0:T(8,128)(2,1)} %hidden_hbm.1, bf16[3584,2048]{1,0:T(8,128)(2,1)} %weight_hbm.1, bf16[2,16,14336]{2,1,0:T(8,128)(2,1)} %select_select_fusion.sent_a_hbm, ...), custom_call_target="tpu_custom_call" | custom-call | flops 15032385536 | bytes 14680064 | tf_op jit(solution)/shard_map/pallas_call | solution.py:612
  66.3 0.0 copy-start
  66.3 0.0 copy-start.1
  66.3 4.2 %copy.16 = bf16[512,3584]{1,0:T(8,128)(2,1)} copy(bf16[512,3584]{1,0:T(8,128)(2,1)} %get-tuple-element.12) | data formatting | bytes 7340032
  70.5 0.0 copy-done
  70.5 0.9 %copy.17 = f32[2,16,7168]{2,1,0:T(8,128)} copy(f32[2,16,7168]{2,1,0:T(8,128)S(1)} %copy-done) | data formatting | bytes 1835008
  71.5 0.0 copy-done.1
  71.5 0.7 copy.18
  (4 shorter events, 0.1 us)
Async XLA Ops:
  3.3 5.4 %copy-start.2 = (f32[8,1024]{1,0:T(8,128)}, f32[8,1024]{1,0:T(8,128)S(1)}, u32[]{:S(2)}) copy-start(f32[8,1024]{1,0:T(8,128)S(1)} %fusion.1.choose_ref) | copy-start | bytes 98308
  66.3 4.2 %copy-start = (f32[2,16,7168]{2,1,0:T(8,128)S(1)}, f32[2,16,7168]{2,1,0:T(8,128)}, u32[]{:S(2)}) copy-start(f32[2,16,7168]{2,1,0:T(8,128)} %get-tuple-element.13) | copy-start | bytes 2752516
  66.3 5.1 %copy-start.1 = (f32[2,16,2048]{2,1,0:T(8,128)S(1)}, f32[2,16,2048]{2,1,0:T(8,128)}, u32[]{:S(2)}) copy-start(f32[2,16,2048]{2,1,0:T(8,128)} %get-tuple-element.14) | copy-start | bytes 786436

commit v2 on v1

--- a/solution.py
+++ b/solution.py
@@ -147,18 +147,24 @@
     grad_hbm,
     hidden_hbm,
     weight_hbm,
-    sent_a_hbm,
-    sent_b_hbm,
-    choose_ref,
-    choose_mine_ref,
-    live_ref,
-    pick_ref,
+    slots_a_hbm,
+    slots_b_hbm,
+    ids_ref,
+    table_ref,
+    seg_ref,
     out_hbm,
     grad_a_ref,
     grad_b_ref,
     grad,
     hid,
     weight,
+    slots_a,
+    slots_b,
+    sent_a,
+    sent_b,
+    choose_ref,
+    choose_mine_ref,
+    live_ref,
     panels_a,
     panels_b,
     own_acc,
@@ -227,6 +233,10 @@
     load_hid = pltpu.make_async_copy(
         hidden_hbm.at[:, lanes(at_t * ff_half, ff_half)], hid, load_sem.at[1]
     )
+    load_slots_a = pltpu.make_async_copy(slots_a_hbm, slots_a, load_sem.at[4])
+    load_slots_b = pltpu.make_async_copy(slots_b_hbm, slots_b, load_sem.at[5])
+    load_slots_b.start()
+    load_slots_a.start()
     load_grad.start()
 
     def load_weight(c):
@@ -257,18 +267,67 @@
         return 0
 
     lax.fori_loop(1, n_all, greet, 0)
+
+    n_slot = slots_a.shape[0]
+    seg = tok // seg_ref.shape[0]
+
+    def slots_of(d):
+        ids = ids_ref[d]
+        slots = jnp.zeros_like(ids)
+        for i in range(table_ref.shape[0]):
+            slots = jnp.where(ids == i, table_ref[i], slots)
+        return slots
+
+    pick = [
+        [
+            jnp.max(
+                jnp.where(slots_of(d) == at_own * n_slot + l, 1.0, 0.0), axis=1, keepdims=True
+            )
+            for l in range(n_slot)
+        ]
+        for d in range(n_data)
+    ]
+    spot = lax.broadcasted_iota(jnp.int32, (1, tok), 1)
+    limit = jnp.zeros((1, tok), jnp.int32)
+    for i in range(tok // seg):
+        limit = jnp.where(spot >= i * seg, seg_ref[i] + i * seg, limit)
+    my_owner = lax.shift_right_logical(slots_of(at_d), 1)
+    my_owner = jnp.where(spot < limit, my_owner, n_own)
+    owner_ids = lax.broadcasted_iota(jnp.int32, (n_own, tok), 0)
+    choose_ref[...] = jnp.where(owner_ids == my_owner, 1.0, 0.0)
+    data_ids = lax.broadcasted_iota(jnp.int32, (n_data, tok), 0)
+    choose_mine_ref[...] = jnp.where(data_ids + at_a * n_data == my_owner, 1.0, 0.0)
+    row_in_seg = lax.broadcasted_iota(jnp.int32, (seg, 128), 0)
+    for i in range(half // seg):
+        live = seg_ref[at_t * (half // seg) + i]
+        live_ref[i * seg : (i + 1) * seg, :] = jnp.where(row_in_seg < live, 1.0, 0.0)
+
+    def choose_slots(slots, sent, size):
+        def step(i, _):
+            place = lanes(i * size, size)
+            for d in range(n_data):
+                total = slots[0, :, place].astype(jnp.float32) * pick[d][0]
+                for l in range(1, n_slot):
+                    total += slots[l, :, place].astype(jnp.float32) * pick[d][l]
+                sent[d, :, place] = total.astype(jnp.bfloat16)
+            return 0
+
+        lax.fori_loop(0, slots.shape[2] // size, step, 0)
+
+    load_slots_b.wait()
+    choose_slots(slots_b, sent_b, 512)
     pl.semaphore_wait(barrier, n_all - 1)
 
     b_copies = [
         pltpu.make_async_copy(
-            sent_b_hbm.at[at_d], panels_b.at[rows(at_d * rank, rank), :], load_sem.at[2]
+            sent_b.at[at_d], panels_b.at[rows(at_d * rank, rank), :], load_sem.at[2]
         )
     ]
     for k in range(1, n_data):
         j = lax.rem(at_d + k, n_data)
         b_copies.append(
             remote(
-                sent_b_hbm.at[j],
+                sent_b.at[j],
                 panels_b.at[rows(at_d * rank, rank), :],
                 b_send.at[k],
                 b_recv.at[k],
@@ -278,10 +337,13 @@
     for copy in b_copies:
         copy.start()
 
+    load_slots_a.wait()
+    choose_slots(slots_a, sent_a, 512)
+
     mine = lanes(at_t * ff_half, ff_half)
     a_copies = [
         pltpu.make_async_copy(
-            sent_a_hbm.at[at_d, :, lanes(at_a * ff + at_t * ff_half, ff_half)],
+            sent_a.at[at_d, :, lanes(at_a * ff + at_t * ff_half, ff_half)],
             panels_a.at[rows(at_own * rank, rank), mine],
             load_sem.at[3],
         )
@@ -291,7 +353,7 @@
         a2, d2 = lax.div(o, n_data), lax.rem(o, n_data)
         a_copies.append(
             remote(
-                sent_a_hbm.at[d2, :, lanes(a2 * ff + at_t * ff_half, ff_half)],
+                sent_a.at[d2, :, lanes(a2 * ff + at_t * ff_half, ff_half)],
                 panels_a.at[rows(at_own * rank, rank), mine],
                 a_send.at[k],
                 a_recv.at[k],
@@ -306,8 +368,6 @@
     load_grad.wait()
 
     pair_dev = dev(at_a, at_d, 1 - at_t)
-    mine_rows = pl.ds(pl.multiple_of(at_t * half, half), half)
-    pair_rows = pl.ds(pl.multiple_of((1 - at_t) * half, half), half)
 
     def pair_copy(c):
         return remote(to_pair.at[c], from_pair.at[c], pair_send.at[c], pair_recv.at[c], pair_dev)
@@ -474,7 +534,7 @@
             j = lax.rem(at_d + k, n_data)
             copies.append(
                 remote(
-                    piece_b.at[j], back_b.at[k], rb_send.at[k], rb_recv.at[k], dev(at_a, j, at_t)
+                    piece_b.at[j], back_b.at[at_d], rb_send.at[k], rb_recv.at[k], dev(at_a, j, at_t)
                 )
             )
         return copies
@@ -495,6 +555,7 @@
                 ).astype(jnp.bfloat16)
             )
         spread_u = jnp.concatenate(parts, axis=1)
+        back_b[at_d] = jnp.zeros_like(back_b[0])
         for i in range(width // 512):
             place = slice(i * 512, (i + 1) * 512)
             wide = jnp.dot(spread_u, grad[:, place], preferred_element_type=jnp.float32)
@@ -514,11 +575,10 @@
     def main(c, _):
         load_weight(c).wait()
         w = weight[pl.ds(pl.multiple_of(c * TILE, TILE), TILE), :]
-        to_pair[c] = lax.dot_general(
-            grad[pair_rows, :], w, NT, preferred_element_type=jnp.float32
-        ).astype(jnp.bfloat16)
+        both = lax.dot_general(grad[...], w, NT, preferred_element_type=jnp.float32)
+        to_pair[c] = jnp.where(at_t == 0, both[half:], both[:half]).astype(jnp.bfloat16)
+        own_acc[c] = jnp.where(at_t == 0, both[:half], both[half:])
         pair_copy(c).start()
-        own_acc[c] = lax.dot_general(grad[mine_rows, :], w, NT, preferred_element_type=jnp.float32)
         for at, event in events.items():
             pl.when(c == min(at, n_tile - 1))(event)
         return 0
@@ -535,25 +595,30 @@
         total += jnp.dot(
             spread_own[...], panels_a[:, lanes(c * TILE, TILE)], preferred_element_type=jnp.float32
         )
-        staged[c] = jnp.where(live_ref[...] > 0, total, 0.0).astype(jnp.bfloat16)
+        for i in range(TILE // 128):
+            place = slice(i * 128, (i + 1) * 128)
+            staged[c, :, place] = jnp.where(live_ref[...] > 0, total[:, place], 0.0).astype(
+                jnp.bfloat16
+            )
         store_copy(c).start()
         return 0
 
     lax.fori_loop(0, n_tile, finish, 0)
 
     wait_all(return_b())
-    n_slot = grad_b_ref.shape[0]
     for l in range(n_slot):
-        total = piece_b[at_d] * pick_ref[at_d, l]
-        for k in range(1, n_data):
-            total += back_b[k] * pick_ref[lax.rem(at_d + n_data - k, n_data), l]
+        total = jnp.zeros_like(piece_b[0])
+        for d in range(n_data):
+            from_here = jnp.where(at_d == d, 1.0, 0.0) * pick[d][l]
+            total += piece_b[d] * from_here
+            total += back_b[d] * (pick[d][l] - from_here)
         grad_b_ref[l] = total
     return_a(False)
     wait_returned()
     for l in range(n_slot):
-        total = back_a[0].astype(jnp.float32) * pick_ref[0, l]
+        total = back_a[0].astype(jnp.float32) * pick[0][l]
         for d in range(1, n_data):
-            total += back_a[d].astype(jnp.float32) * pick_ref[d, l]
+            total += back_a[d].astype(jnp.float32) * pick[d][l]
         grad_a_ref[l] = total
 
     def drain(c, _):
@@ -584,44 +649,33 @@
     half = tok // n_pair
     ff_half = ff // n_pair
     n_tile = ff // TILE
-    at_data = lax.axis_index("dp")
-    at_pair = lax.axis_index("tensor")
-    at_own = lax.axis_index("adapter") * n_data + at_data
-    token_slot = lookup(token_adapter_table, adapter_slot_table).reshape(n_data, tok)
-    my_ids = at_own * n_slot + jnp.arange(n_slot, dtype=jnp.int32)
-    pick = jnp.any(token_slot[:, :, None] == my_ids[None, None, :], axis=1)
-    sent_a = jnp.zeros((n_data, rank, ff_all), jnp.bfloat16)
-    sent_b = jnp.zeros((n_data, rank, width), jnp.bfloat16)
-    for l in range(n_slot):
-        sent_a = jnp.where(pick[:, l, None, None], adapter_input_panels[l][None], sent_a)
-        sent_b = jnp.where(pick[:, l, None, None], adapter_output_panels[l][None], sent_b)
-    seg = tok // segment_live_tokens.shape[0]
-    seg_pos = jnp.arange(seg, dtype=jnp.int32)
-    live = (seg_pos[None, :] < segment_live_tokens[:, None]).reshape(tok)
-    my_owner = lax.dynamic_index_in_dim(token_slot, at_data, 0, False) // n_slot
-    owner_ids = jnp.arange(n_own, dtype=jnp.int32)
-    choose = ((my_owner[None, :] == owner_ids[:, None]) & live[None, :]).astype(jnp.float32)
-    choose_mine = lax.dynamic_slice_in_dim(choose, at_own - at_data, n_data, 0)
-    live_half = lax.dynamic_slice_in_dim(live, at_pair * half, half, 0).astype(jnp.float32)[:, None]
     anywhere = pl.BlockSpec(memory_space=pl.ANY)
     vmem = pl.BlockSpec(memory_space=pltpu.VMEM)
+    smem = pl.BlockSpec(memory_space=pltpu.SMEM)
     dma = pltpu.SemaphoreType.DMA
     bf16, f32 = jnp.bfloat16, jnp.float32
     ff_out = ff_all // n_pair
     n_back = n_adapter // n_pair * n_data * n_pair
-    return pl.pallas_call(
+    outs = pl.pallas_call(
         functools.partial(fused_kernel, (n_adapter, n_data, n_pair, rank)),
         out_shape=(
             jax.ShapeDtypeStruct((half, ff), bf16),
             jax.ShapeDtypeStruct((n_slot, rank, ff_out), f32),
             jax.ShapeDtypeStruct((n_slot, rank, width), f32),
         ),
-        in_specs=[anywhere] * 5 + [vmem, vmem, vmem, pl.BlockSpec(memory_space=pltpu.SMEM)],
+        in_specs=[anywhere] * 5 + [vmem, smem, smem],
         out_specs=(anywhere, vmem, vmem),
         scratch_shapes=[
             pltpu.VMEM((tok, width), bf16),
             pltpu.VMEM((tok, ff_half), bf16),
             pltpu.VMEM((ff, width), bf16),
+            pltpu.VMEM((n_slot, rank, ff_all), bf16),
+            pltpu.VMEM((n_slot, rank, width), bf16),
+            pltpu.VMEM((n_data, rank, ff_all), bf16),
+            pltpu.VMEM((n_data, rank, width), bf16),
+            pltpu.VMEM((n_own, tok), f32),
+            pltpu.VMEM((n_data, tok), f32),
+            pltpu.VMEM((half, 128), f32),
             pltpu.VMEM((n_own * rank, ff), bf16),
             pltpu.VMEM((n_data * rank, width), bf16),
             pltpu.VMEM((n_tile, half, TILE), f32),
@@ -637,7 +691,7 @@
             pltpu.VMEM((n_data, rank, ff_out), bf16),
             pltpu.VMEM((n_data, rank, width), f32),
             pltpu.VMEM((n_data, rank, width), f32),
-            dma((4,)),
+            dma((6,)),
             dma((n_tile,)),
             dma((n_tile,)),
             dma((n_own,)),
@@ -666,13 +720,44 @@
         output_gradient,
         hidden,
         frozen_down_weight,
-        sent_a,
-        sent_b,
-        choose,
-        choose_mine,
-        live_half,
-        pick.astype(jnp.float32),
-    )
+        adapter_input_panels,
+        adapter_output_panels,
+        token_adapter_table.reshape(n_data, 1, tok),
+        adapter_slot_table,
+        segment_live_tokens,
+    )
+    return tuple(copy_out(outs))
+
+
+def copy_kernel(n_arrays, n_cuts, *refs):
+    copies = []
+    sems = refs[2 * n_arrays]
+    for a in range(n_arrays):
+        src, dst = refs[a], refs[n_arrays + a]
+        rows = src.shape[0] // n_cuts[a]
+        for i in range(n_cuts[a]):
+            place = slice(i * rows, (i + 1) * rows)
+            copies.append(
+                pltpu.make_async_copy(src.at[place], dst.at[place], sems.at[len(copies)])
+            )
+    for copy in copies:
+        copy.start()
+    for copy in copies:
+        copy.wait()
+
+
+def copy_out(arrays):
+    anywhere = pl.BlockSpec(memory_space=pl.ANY)
+    cuts = [8 if array.ndim == 2 else array.shape[0] for array in arrays]
+    size = sum(array.size * array.dtype.itemsize for array in arrays)
+    return pl.pallas_call(
+        functools.partial(copy_kernel, len(arrays), cuts),
+        out_shape=[jax.ShapeDtypeStruct(array.shape, array.dtype) for array in arrays],
+        in_specs=[anywhere] * len(arrays),
+        out_specs=[anywhere] * len(arrays),
+        scratch_shapes=[pltpu.SemaphoreType.DMA((sum(cuts),))],
+        cost_estimate=pl.CostEstimate(flops=0, bytes_accessed=2 * size, transcendentals=0),
+    )(*arrays)
 
 
 def fits_kernel(hidden, adapter_input_panels):
@@ -691,6 +776,7 @@
         and ff // TILE > 11
         and hidden.shape[0] == n_sum * 128
         and n_adapter * n_data * rank <= 256
+        and adapter_input_panels.shape[2] % 512 == 0
     )
 
 

time: 72.4 us -> 202 us (2.79)
  Pallas kernels: 57.6 us -> 201 us
  local copies, waits for them, and re-layouts: 9.59 us -> 0 us
  other arithmetic: 4.25 us -> 0 us
    pallas_call x0 -> x1, Pallas kernels: none -> 148 us  [copy_out(): pl.pallas_call(functools.partial(copy_kernel, len(arrays), cuts), out_sha...]
    unnamed x9 -> x0, local copies, waits for them, and re-layouts: 5.84 us -> none
    pallas_call x1, Pallas kernels: 57.6 us -> 52.8 us  [fused_on_device(): pl.pallas_call(functools.partial(fused_kernel, (n_adapter, n_data, n_pair...]
    broadcast_in_dim x3 -> x0, local copies, waits for them, and re-layouts: 2.95 us -> none  [the longest x1 1.22 us: fused_on_device(): jnp.where(pick[:, l, None, None], adapter_input_panels[l][None], sent_a)]
where the time goes in v2:
time: 202 us
  Pallas kernels  201 us (100%)
    pallas_call x1, Pallas kernels, copy_out(): pl.pallas_call(functools.partial(copy_kernel, len(arrays), cuts), out_sha...  148 us
    pallas_call x1, Pallas kernels, fused_on_device(): pl.pallas_call(functools.partial(fused_kernel, (n_adapter, n_data, n_pair...  52.8 us

profile of v2, /device:TPU:0, one launch (start us, length us, event | category | flops | bytes accessed | tf_op | source)
XLA Modules:
  0.0 201.5 jit_solution(7143331904780597770)
XLA Ops:
  0.6 52.8 %shard_map.103 = (bf16[512,3584]{1,0:T(8,128)(2,1)}, f32[2,16,7168]{2,1,0:T(8,128)}, f32[2,16,2048]{2,1,0:T(8,128)}) custom-call(bf16[1024,2048]{1,0:T(8,128)(2,1)} %grad_hbm.1, bf16[1024,3584]{1,0:T(8,128)(2,1)} %hidden_hbm.1, bf16[3584,2048]{1,0:T(8,128)(2,1)} %weight_hbm.1, bf16[2,16,14336]{2,1,0:T(8,128)(2,1)} %slots_a_hbm.1, ...), custom_call_target="tpu_custom_call" | custom-call | flops 15032385536 | bytes 14680064 | tf_op jit(solution)/shard_map/pallas_call | solution.py:659
  53.4 148.1 %shard_map.104 = (bf16[512,3584]{1,0:T(8,128)(2,1)}, f32[2,16,7168]{2,1,0:T(8,128)}, f32[2,16,2048]{2,1,0:T(8,128)}) custom-call(bf16[512,3584]{1,0:T(8,128)(2,1)} %get-tuple-element.6.refs_0_, f32[2,16,7168]{2,1,0:T(8,128)} %get-tuple-element.7.refs_1_, f32[2,16,2048]{2,1,0:T(8,128)} %get-tuple-element.8.refs_2_), custom_call_target="tpu_custom_call" | custom-call | bytes 9699328 | tf_op jit(solution)/shard_map/pallas_call | solution.py:753

commit v3 on v2

--- a/solution.py
+++ b/solution.py
@@ -218,6 +218,8 @@
     def dev(a, d, t):
         return (at_g, a, d, t)
 
+    far_first = sorted(range(1, n_own), key=lambda k: -min(k, n_own - k))
+
     def remote(src, dst, send, recv, to):
         return pltpu.make_async_remote_copy(
             src_ref=src, dst_ref=dst, send_sem=send, recv_sem=recv, device_id=to, device_id_type=MESH
@@ -287,6 +289,70 @@
         ]
         for d in range(n_data)
     ]
+    def choose_slots(slots, sent, size):
+        def step(i, _):
+            place = lanes(i * size, size)
+            for d in range(n_data):
+                total = slots[0, :, place].astype(jnp.float32) * pick[d][0]
+                for l in range(1, n_slot):
+                    total += slots[l, :, place].astype(jnp.float32) * pick[d][l]
+                sent[d, :, place] = total.astype(jnp.bfloat16)
+            return 0
+
+        lax.fori_loop(0, slots.shape[2] // size, step, 0)
+
+    pl.semaphore_wait(barrier, n_all - 1)
+    load_slots_b.wait()
+    choose_slots(slots_b, sent_b, 512)
+    b_copies = [
+        pltpu.make_async_copy(
+            sent_b.at[at_d], panels_b.at[rows(at_d * rank, rank), :], load_sem.at[2]
+        )
+    ]
+    for k in range(1, n_data):
+        j = lax.rem(at_d + k, n_data)
+        b_copies.append(
+            remote(
+                sent_b.at[j],
+                panels_b.at[rows(at_d * rank, rank), :],
+                b_send.at[k],
+                b_recv.at[k],
+                dev(at_a, j, at_t),
+            )
+        )
+    for copy in b_copies:
+        copy.start()
+
+    load_slots_a.wait()
+    choose_slots(slots_a, sent_a, ff_half)
+
+    mine = lanes(at_t * ff_half, ff_half)
+    a_copies = [
+        pltpu.make_async_copy(
+            sent_a.at[at_d, :, lanes(at_a * ff + at_t * ff_half, ff_half)],
+            panels_a.at[rows(at_own * rank, rank), mine],
+            load_sem.at[3],
+        )
+    ]
+    for k in far_first:
+        o = lax.rem(at_own + k, n_own)
+        a2, d2 = lax.div(o, n_data), lax.rem(o, n_data)
+        a_copies.append(
+            remote(
+                sent_a.at[d2, :, lanes(a2 * ff + at_t * ff_half, ff_half)],
+                panels_a.at[rows(at_own * rank, rank), mine],
+                a_send.at[k],
+                a_recv.at[k],
+                dev(a2, d2, at_t),
+            )
+        )
+    for copy in a_copies:
+        copy.start()
+    lax.fori_loop(2, 6, start_weight, 0)
+    load_hid.start()
+    lax.fori_loop(6, n_tile, start_weight, 0)
+    load_grad.wait()
+
     spot = lax.broadcasted_iota(jnp.int32, (1, tok), 1)
     limit = jnp.zeros((1, tok), jnp.int32)
     for i in range(tok // seg):
@@ -302,70 +368,6 @@
         live = seg_ref[at_t * (half // seg) + i]
         live_ref[i * seg : (i + 1) * seg, :] = jnp.where(row_in_seg < live, 1.0, 0.0)
 
-    def choose_slots(slots, sent, size):
-        def step(i, _):
-            place = lanes(i * size, size)
-            for d in range(n_data):
-                total = slots[0, :, place].astype(jnp.float32) * pick[d][0]
-                for l in range(1, n_slot):
-                    total += slots[l, :, place].astype(jnp.float32) * pick[d][l]
-                sent[d, :, place] = total.astype(jnp.bfloat16)
-            return 0
-
-        lax.fori_loop(0, slots.shape[2] // size, step, 0)
-
-    load_slots_b.wait()
-    choose_slots(slots_b, sent_b, 512)
-    pl.semaphore_wait(barrier, n_all - 1)
-
-    b_copies = [
-        pltpu.make_async_copy(
-            sent_b.at[at_d], panels_b.at[rows(at_d * rank, rank), :], load_sem.at[2]
-        )
-    ]
-    for k in range(1, n_data):
-        j = lax.rem(at_d + k, n_data)
-        b_copies.append(
-            remote(
-                sent_b.at[j],
-                panels_b.at[rows(at_d * rank, rank), :],
-                b_send.at[k],
-                b_recv.at[k],
-                dev(at_a, j, at_t),
-            )
-        )
-    for copy in b_copies:
-        copy.start()
-
-    load_slots_a.wait()
-    choose_slots(slots_a, sent_a, 512)
-
-    mine = lanes(at_t * ff_half, ff_half)
-    a_copies = [
-        pltpu.make_async_copy(
-            sent_a.at[at_d, :, lanes(at_a * ff + at_t * ff_half, ff_half)],
-            panels_a.at[rows(at_own * rank, rank), mine],
-            load_sem.at[3],
-        )
-    ]
-    for k in range(1, n_own):
-        o = lax.rem(at_own + k, n_own)
-        a2, d2 = lax.div(o, n_data), lax.rem(o, n_data)
-        a_copies.append(
-            remote(
-                sent_a.at[d2, :, lanes(a2 * ff + at_t * ff_half, ff_half)],
-                panels_a.at[rows(at_own * rank, rank), mine],
-                a_send.at[k],
-                a_recv.at[k],
-                dev(a2, d2, at_t),
-            )
-        )
-    for copy in a_copies:
-        copy.start()
-    lax.fori_loop(2, 6, start_weight, 0)
-    load_hid.start()
-    lax.fori_loop(6, n_tile, start_weight, 0)
-    load_grad.wait()
 
     pair_dev = dev(at_a, at_d, 1 - at_t)
 
@@ -380,24 +382,24 @@
         q = lax.rem(at_sum + k, n_sum)
         return q, dev(lax.div(q, n_pair), at_d, lax.rem(q, n_pair))
 
-    def scatter_copies(w):
+    def scatter_copies():
         copies = []
         for k in range(1, n_sum):
             q, to = sum_peer(k)
             copies.append(
                 remote(
-                    part.at[w, q], part_in.at[w, k], rs_send.at[w, k], rs_recv.at[w, k], to
+                    part.at[q], part_in.at[k], rs_send.at[k], rs_recv.at[k], to
                 )
             )
         return copies
 
-    def gather_copies(w):
+    def gather_copies():
         copies = []
         for k in range(1, n_sum):
             _, to = sum_peer(k)
             copies.append(
                 remote(
-                    low.at[w, at_sum], low.at[w, at_sum], ag_send.at[w, k], ag_recv.at[w, k], to
+                    low.at[at_sum], low.at[at_sum], ag_send.at[k], ag_recv.at[k], to
                 )
             )
         return copies
@@ -412,7 +414,7 @@
 
     def store_part(w, i, value):
         for s in range(TILE // tok_piece):
-            part[w, i * (TILE // tok_piece) + s] = value[:, s * tok_piece : (s + 1) * tok_piece]
+            part[i * (TILE // tok_piece) + s, w] = value[:, s * tok_piece : (s + 1) * tok_piece]
 
     def part_v():
         wait_all(b_copies)
@@ -428,10 +430,10 @@
             return 0
 
         lax.fori_loop(0, tok // TILE, step, 0)
-        start_all(scatter_copies(1))
 
     def part_u():
         wait_all(a_copies)
+        load_hid.wait()
         forward.start()
 
         def step(i, _):
@@ -447,26 +449,25 @@
             return 0
 
         lax.fori_loop(0, tok // TILE, step, 0)
-        start_all(scatter_copies(0))
-
-    def sum_low(w):
-        wait_all(scatter_copies(w))
-        total = part[w, at_sum]
+        start_all(scatter_copies())
+
+    def sum_low():
+        wait_all(scatter_copies())
+        total = part[at_sum]
         for k in range(1, n_sum):
-            total += part_in[w, k]
-        low[w, at_sum] = total.astype(jnp.bfloat16)
-        start_all(gather_copies(w))
+            total += part_in[k]
+        low[at_sum] = total.astype(jnp.bfloat16)
+        start_all(gather_copies())
 
     def use_v():
-        wait_all(gather_copies(1))
+        wait_all(gather_copies())
         for i in range(n_sum):
-            value = low[1, i].astype(jnp.float32) * adapter_scale
+            value = low[i, 1].astype(jnp.float32) * adapter_scale
             place = slice(i * tok_piece, (i + 1) * tok_piece)
             for o in range(n_own):
                 spread[o * rank : (o + 1) * rank, place] = (
                     value * choose_ref[o : o + 1, place]
                 ).astype(jnp.bfloat16)
-        load_hid.wait()
 
         def step(i, _):
             place = lanes(i * TILE, TILE)
@@ -476,10 +477,10 @@
             return 0
 
         lax.fori_loop(0, ff_half // TILE, step, 0)
+        return_a(True)
         spread_own[...] = jnp.transpose(
             spread[:, lanes(at_t * half, half)].astype(jnp.float32)
         ).astype(jnp.bfloat16)
-        return_a(True)
 
     ratio = n_adapter // n_pair
     core = lax.div(at_a, ratio)
@@ -498,7 +499,7 @@
         )
 
     def return_a(start):
-        for k in range(1, n_own):
+        for k in far_first:
             if start:
                 return_copy(k).start()
             else:
@@ -540,10 +541,9 @@
         return copies
 
     def use_u():
-        wait_all(gather_copies(0))
         parts = []
         for i in range(n_sum):
-            value = low[0, i].astype(jnp.float32) * adapter_scale
+            value = low[i, 0].astype(jnp.float32) * adapter_scale
             place = slice(i * tok_piece, (i + 1) * tok_piece)
             parts.append(
                 jnp.concatenate(
@@ -563,14 +563,7 @@
                 piece_b[j, :, place] = wide[j * rank : (j + 1) * rank]
         start_all(return_b())
 
-    events = {
-        1: part_v,
-        3: lambda: sum_low(1),
-        5: use_v,
-        7: part_u,
-        9: lambda: sum_low(0),
-        11: use_u,
-    }
+    events = {3: part_v, 5: part_u, 7: sum_low, 9: use_v, 10: use_u}
 
     def main(c, _):
         load_weight(c).wait()
@@ -682,9 +675,9 @@
             pltpu.VMEM((n_tile, half, TILE), bf16),
             pltpu.VMEM((n_tile, half, TILE), bf16),
             pltpu.VMEM((n_tile, half, TILE), bf16),
-            pltpu.VMEM((2, n_sum, rank, tok // n_sum), f32),
-            pltpu.VMEM((2, n_sum, rank, tok // n_sum), f32),
-            pltpu.VMEM((2, n_sum, rank, tok // n_sum), bf16),
+            pltpu.VMEM((n_sum, 2, rank, tok // n_sum), f32),
+            pltpu.VMEM((n_sum, 2, rank, tok // n_sum), f32),
+            pltpu.VMEM((n_sum, 2, rank, tok // n_sum), bf16),
             pltpu.VMEM((n_own * rank, tok), bf16),
             pltpu.VMEM((half, n_own * rank), bf16),
             pltpu.VMEM((n_own * rank, ff_half), bf16),
@@ -701,10 +694,10 @@
             dma((n_tile,)),
             dma((n_tile,)),
             dma((2,)),
-            dma((2, n_sum)),
-            dma((2, n_sum)),
-            dma((2, n_sum)),
-            dma((2, n_sum)),
+            dma((n_sum,)),
+            dma((n_sum,)),
+            dma((n_sum,)),
+            dma((n_sum,)),
             dma((n_own,)),
             dma((n_back,)),
             dma((n_data,)),
@@ -730,20 +723,27 @@
 
 
 def copy_kernel(n_arrays, n_cuts, *refs):
-    copies = []
-    sems = refs[2 * n_arrays]
+    held = refs[2 * n_arrays : 3 * n_arrays]
+    in_sem, out_sem = refs[3 * n_arrays :]
+    loads, stores = [], []
     for a in range(n_arrays):
         src, dst = refs[a], refs[n_arrays + a]
         rows = src.shape[0] // n_cuts[a]
         for i in range(n_cuts[a]):
-            place = slice(i * rows, (i + 1) * rows)
-            copies.append(
-                pltpu.make_async_copy(src.at[place], dst.at[place], sems.at[len(copies)])
-            )
-    for copy in copies:
-        copy.start()
-    for copy in copies:
-        copy.wait()
+            place, at = slice(i * rows, (i + 1) * rows), len(loads)
+            loads.append(
+                pltpu.make_async_copy(src.at[place], held[a].at[place], in_sem.at[at])
+            )
+            stores.append(
+                pltpu.make_async_copy(held[a].at[place], dst.at[place], out_sem.at[at])
+            )
+    for load in loads:
+        load.start()
+    for load, store in zip(loads, stores):
+        load.wait()
+        store.start()
+    for store in stores:
+        store.wait()
 
 
 def copy_out(arrays):
@@ -755,7 +755,9 @@
         out_shape=[jax.ShapeDtypeStruct(array.shape, array.dtype) for array in arrays],
         in_specs=[anywhere] * len(arrays),
         out_specs=[anywhere] * len(arrays),
-        scratch_shapes=[pltpu.SemaphoreType.DMA((sum(cuts),))],
+        scratch_shapes=[pltpu.VMEM(array.shape, array.dtype) for array in arrays]
+        + [pltpu.SemaphoreType.DMA((sum(cuts),))] * 2,
+        compiler_params=pltpu.CompilerParams(vmem_limit_bytes=60 * 1024 * 1024),
         cost_estimate=pl.CostEstimate(flops=0, bytes_accessed=2 * size, transcendentals=0),
     )(*arrays)
 

time: 202 us -> 47.9 us (0.24)
  Pallas kernels: 201 us -> 46.7 us
    pallas_call x1, Pallas kernels: 148 us -> 4.26 us  [copy_out(): pl.pallas_call(functools.partial(copy_kernel, len(arrays), cuts), out_sha...]
    pallas_call x1, Pallas kernels: 52.8 us -> 42.5 us  [fused_on_device(): pl.pallas_call(functools.partial(fused_kernel, (n_adapter, n_data, n_pair...]
where the time goes in v3:
time: 47.9 us; the launch traced here: 47.4 us
  Pallas kernels  46.7 us (97%)
  between operations  0.64 us (1%)
    pallas_call x1, Pallas kernels, fused_on_device(): pl.pallas_call(functools.partial(fused_kernel, (n_adapter, n_data, n_pair...  42.5 us
    pallas_call x1, Pallas kernels, copy_out(): pl.pallas_call(functools.partial(copy_kernel, len(arrays), cuts), out_sha...  4.26 us

profile of v3, /device:TPU:0, one launch (start us, length us, event | category | flops | bytes accessed | tf_op | source)
XLA Modules:
  0.0 47.4 jit_solution(14316346767684824498)
XLA Ops:
  0.6 42.5 %shard_map.103 = (bf16[512,3584]{1,0:T(8,128)(2,1)}, f32[2,16,7168]{2,1,0:T(8,128)}, f32[2,16,2048]{2,1,0:T(8,128)}) custom-call(bf16[1024,2048]{1,0:T(8,128)(2,1)} %grad_hbm.1, bf16[1024,3584]{1,0:T(8,128)(2,1)} %hidden_hbm.1, bf16[3584,2048]{1,0:T(8,128)(2,1)} %weight_hbm.1, bf16[2,16,14336]{2,1,0:T(8,128)(2,1)} %slots_a_hbm.1, ...), custom_call_target="tpu_custom_call" | custom-call | flops 15032385536 | bytes 14680064 | tf_op jit(solution)/shard_map/pallas_call | solution.py:652
  43.1 4.3 %shard_map.104 = (bf16[512,3584]{1,0:T(8,128)(2,1)}, f32[2,16,7168]{2,1,0:T(8,128)}, f32[2,16,2048]{2,1,0:T(8,128)}) custom-call(bf16[512,3584]{1,0:T(8,128)(2,1)} %get-tuple-element.6.refs_0_, f32[2,16,7168]{2,1,0:T(8,128)} %get-tuple-element.7.refs_1_, f32[2,16,2048]{2,1,0:T(8,128)} %get-tuple-element.8.refs_2_), custom_call_target="tpu_custom_call" | custom-call | bytes 9699328 | tf_op jit(solution)/shard_map/pallas_call | solution.py:753

commit v4 on v3

--- a/solution.py
+++ b/solution.py
@@ -748,7 +748,7 @@
 
 def copy_out(arrays):
     anywhere = pl.BlockSpec(memory_space=pl.ANY)
-    cuts = [8 if array.ndim == 2 else array.shape[0] for array in arrays]
+    cuts = [4 if array.ndim == 2 else array.shape[0] for array in arrays]
     size = sum(array.size * array.dtype.itemsize for array in arrays)
     return pl.pallas_call(
         functools.partial(copy_kernel, len(arrays), cuts),

time: 47.9 us -> 47.5 us (level)
  no operation moved by 1% of the time
where the time goes in v4:
time: 47.5 us; the launch traced here: 46.9 us
  Pallas kernels  46.3 us (97%)
  between operations  0.64 us (1%)
    pallas_call x1, Pallas kernels, fused_on_device(): pl.pallas_call(functools.partial(fused_kernel, (n_adapter, n_data, n_pair...  42.5 us
    pallas_call x1, Pallas kernels, copy_out(): pl.pallas_call(functools.partial(copy_kernel, len(arrays), cuts), out_sha...  3.78 us

profile of v4, /device:TPU:0, one launch (start us, length us, event | category | flops | bytes accessed | tf_op | source)
XLA Modules:
  0.0 46.9 jit_solution(6272296448548899411)
XLA Ops:
  0.6 42.5 %shard_map.103 = (bf16[512,3584]{1,0:T(8,128)(2,1)}, f32[2,16,7168]{2,1,0:T(8,128)}, f32[2,16,2048]{2,1,0:T(8,128)}) custom-call(bf16[1024,2048]{1,0:T(8,128)(2,1)} %grad_hbm.1, bf16[1024,3584]{1,0:T(8,128)(2,1)} %hidden_hbm.1, bf16[3584,2048]{1,0:T(8,128)(2,1)} %weight_hbm.1, bf16[2,16,14336]{2,1,0:T(8,128)(2,1)} %slots_a_hbm.1, ...), custom_call_target="tpu_custom_call" | custom-call | flops 15032385536 | bytes 14680064 | tf_op jit(solution)/shard_map/pallas_call | solution.py:652
  43.1 3.8 %shard_map.104 = (bf16[512,3584]{1,0:T(8,128)(2,1)}, f32[2,16,7168]{2,1,0:T(8,128)}, f32[2,16,2048]{2,1,0:T(8,128)}) custom-call(bf16[512,3584]{1,0:T(8,128)(2,1)} %get-tuple-element.6.refs_0_, f32[2,16,7168]{2,1,0:T(8,128)} %get-tuple-element.7.refs_1_, f32[2,16,2048]{2,1,0:T(8,128)} %get-tuple-element.8.refs_2_), custom_call_target="tpu_custom_call" | custom-call | bytes 9699328 | tf_op jit(solution)/shard_map/pallas_call | solution.py:753
